TPU v7x, 32 devices: a whole 2x2x4 slice. The times are simulated.
32 devices in a mesh: section: 2 (over core), head: 4 (over z), blk: 4 (over y, x).
Axes of the slice: x: 2, y: 2, z: 4, core: 2. Of those that a mesh axis runs over, the one named last changes fastest.
Arguments:
- section_input: bfloat16 [2, 8, 256, 1536], P('section', 'blk')
- modulation: bfloat16 [2, 8, 2, 1536], P('section', 'blk'), may hold values from -3 to 3
- attn_gate: bfloat16 [2, 8, 1536], P('section', 'blk'), may hold values from -12 to 12
- qkv_weight: bfloat16 [2, 1536, 3, 1536], P('section', None, None, 'head'), may hold values from -0.15625 to 0.15625
- out_weight: bfloat16 [2, 1536, 1536], P('section', 'head'), may hold values from -0.15625 to 0.15625
- kv_cache: bfloat16 [2, 8, 256, 4, 2, 1536], P('section', None, 'blk', None, None, 'head'), may hold values from -9 to 9
- text_kv: bfloat16 [2, 8, 154, 2, 1536], P('section', 'blk', None, None, 'head')
- text_len: int32 [8], P('blk'), may hold values from 4 to 154, as said below
- patch_order: int32 [4, 4], replicated, may hold values from 0 to 3, each once within a row
- final_mod: bfloat16 [8, 2, 1536], P('blk'), may hold values from -3 to 3
- final_weight: bfloat16 [1536, 64], replicated, may hold values from -0.15625 to 0.15625
- latent: float32 [4, 128, 128], P('blk', 'section'), may hold values from -6 to 6
Outputs:
- section_output: bfloat16 [2, 8, 256, 1536], P('section', 'blk', None, 'head')
- cache_patch: bfloat16 [2, 8, 256, 2, 1536], P('section', None, 'blk', None, 'head')
- latent_next: float32 [4, 128, 128], P('blk', 'section')
Inputs may be any that keep to these rules, and one draw needn't show every extreme that they name: `text_len`: sequence 0 uses all 154 text positions. `patch_order`: each row is a permutation of the 4 patches.
All inputs are finite; a program needn't handle non-finite values.
Results may differ from a plain program's by a relative error of at most 0.0092.
Values may be sent and summed in bfloat16 or wider, within the bound.
A program may use at most 128 MiB of HBM per device.

v0:
```python
import jax
import jax.numpy as jnp
from jax import lax
from jax.sharding import PartitionSpec as P

HEAD_DIM = 64
norm_eps = 1e-06
guidance = 4.0
euler_step = -0.25


def passed_along(shard, axis, by):
    devices = lax.axis_size(axis)
    return lax.ppermute(shard, axis, [(i, (i + by) % devices) for i in range(devices)])


def layer_norm(values):
    row_mean = jnp.mean(values, axis=-1, keepdims=True)
    centered = values - row_mean
    row_var = jnp.mean(centered * centered, axis=-1, keepdims=True)
    return centered / jnp.sqrt(row_var + norm_eps)


def piece_scores(query_heads, key_piece, counted_piece):
    seq_dev = key_piece.shape[0]
    head_count = query_heads.shape[2]
    key_heads = key_piece.reshape(seq_dev, -1, head_count, HEAD_DIM)
    scores = jnp.einsum(
        "sqhd,skhd->shqk", query_heads, key_heads, preferred_element_type=jnp.float32
    ) * HEAD_DIM ** (-0.5)
    if counted_piece is not None:
        scores = jnp.where(counted_piece[:, None, None, :], scores, -1e30)
    return scores


def piece_values(probs_piece, value_piece, head_count):
    seq_dev = value_piece.shape[0]
    value_heads = value_piece.reshape(seq_dev, -1, head_count, HEAD_DIM)
    return jnp.einsum(
        "shqk,skhd->sqhd", probs_piece, value_heads, preferred_element_type=jnp.float32
    )


def shards(
    section_input,
    modulation,
    attn_gate,
    qkv_weight,
    out_weight,
    kv_cache,
    text_kv,
    text_len,
    patch_order,
    final_mod,
    final_weight,
    latent,
):
    section_index = lax.axis_index("section")
    seq_patch = jnp.repeat(
        lax.dynamic_index_in_dim(patch_order, section_index, 1, keepdims=False), 2
    )
    hidden_in = section_input[0]
    seq_dev, patch_rows, model_width = hidden_in.shape
    own_patch = lax.dynamic_slice_in_dim(seq_patch, lax.axis_index("blk") * seq_dev, seq_dev, 0)
    hidden_wide = hidden_in.astype(jnp.float32)
    shift_scale = modulation[0].astype(jnp.float32)
    normed = (layer_norm(hidden_wide) * (1.0 + shift_scale[:, 1:2]) + shift_scale[:, 0:1]).astype(
        jnp.bfloat16
    )
    group_width = qkv_weight.shape[3]
    projected = jnp.dot(
        normed.reshape(seq_dev * patch_rows, model_width),
        qkv_weight[0].reshape(model_width, 3 * group_width),
        preferred_element_type=jnp.float32,
    ).astype(jnp.bfloat16)
    projected = projected.reshape(seq_dev, patch_rows, 3, group_width)
    queries = projected[:, :, 0]
    key_new = projected[:, :, 1]
    value_new = projected[:, :, 2]
    fresh_kv = jnp.stack([key_new, value_new], axis=2)
    refreshed = lax.all_to_all(fresh_kv, "blk", split_axis=1, concat_axis=0, tiled=True)
    local_cache = kv_cache[0]
    patch_count = local_cache.shape[2]
    fetched = lax.all_to_all(local_cache, "blk", split_axis=0, concat_axis=1, tiled=True)
    keep_patch = jnp.arange(patch_count, dtype=jnp.int32)[None, :] != own_patch[:, None]
    stale_counted = jnp.tile(keep_patch, (1, patch_rows))
    stale_keys = fetched[:, :, :, 0].reshape(seq_dev, -1, group_width)
    stale_values = fetched[:, :, :, 1].reshape(seq_dev, -1, group_width)
    text_local = text_kv[0]
    text_count = text_local.shape[1]
    text_counted = jnp.arange(text_count, dtype=jnp.int32)[None, :] < text_len[:, None]
    head_count = group_width // HEAD_DIM
    query_heads = queries.reshape(seq_dev, patch_rows, head_count, HEAD_DIM)
    text_scores = piece_scores(query_heads, text_local[:, :, 0], text_counted)
    fresh_scores = piece_scores(query_heads, key_new, None)
    stale_scores = piece_scores(query_heads, stale_keys, stale_counted)
    row_max = jnp.maximum(
        jnp.maximum(
            jnp.max(text_scores, axis=-1, keepdims=True),
            jnp.max(fresh_scores, axis=-1, keepdims=True),
        ),
        jnp.max(stale_scores, axis=-1, keepdims=True),
    )
    text_weights = jnp.exp(text_scores - row_max)
    fresh_weights = jnp.exp(fresh_scores - row_max)
    stale_weights = jnp.exp(stale_scores - row_max)
    total = (
        jnp.sum(text_weights, axis=-1, keepdims=True)
        + jnp.sum(fresh_weights, axis=-1, keepdims=True)
        + jnp.sum(stale_weights, axis=-1, keepdims=True)
    )
    text_probs = (text_weights / total).astype(jnp.bfloat16)
    fresh_probs = (fresh_weights / total).astype(jnp.bfloat16)
    stale_probs = (stale_weights / total).astype(jnp.bfloat16)
    attended_wide = (
        piece_values(text_probs, text_local[:, :, 1], head_count)
        + piece_values(fresh_probs, value_new, head_count)
        + piece_values(stale_probs, stale_values, head_count)
    )
    attended = attended_wide.astype(jnp.bfloat16)
    partial_value = jnp.dot(
        attended.reshape(seq_dev * patch_rows, group_width),
        out_weight[0],
        preferred_element_type=jnp.float32,
    )
    gate_wide = attn_gate[0].astype(jnp.float32)[:, None, :]
    share_width = model_width // lax.axis_size("head")
    share_start = lax.axis_index("head") * share_width
    half_rows = patch_rows // 2
    share_sum = lax.psum_scatter(
        partial_value.reshape(seq_dev, patch_rows, model_width).astype(jnp.bfloat16),
        "head",
        scatter_dimension=2,
        tiled=True,
    ).astype(jnp.float32)
    own_hidden = lax.dynamic_slice_in_dim(hidden_wide, share_start, share_width, 2)
    own_gate = lax.dynamic_slice_in_dim(gate_wide, share_start, share_width, 2)
    layer_out = (own_hidden + own_gate * share_sum).astype(jnp.bfloat16)
    received = passed_along(layer_out, "section", 1)
    last_layer = jnp.where(section_index == 0, received, layer_out)
    last_half = lax.dynamic_slice_in_dim(last_layer, section_index * half_rows, half_rows, 1)
    final_rows = lax.all_gather(last_half, "head", axis=2, tiled=True)
    final_shift = final_mod.astype(jnp.float32)
    final_normed = (
        layer_norm(final_rows.astype(jnp.float32)) * (1.0 + final_shift[:, 1:2])
        + final_shift[:, 0:1]
    ).astype(jnp.bfloat16)
    velocity = jnp.dot(
        final_normed.reshape(seq_dev * half_rows, model_width),
        final_weight,
        preferred_element_type=jnp.float32,
    )
    velocity = velocity.reshape(seq_dev // 2, 2, -1)
    guided = velocity[:, 1] + guidance * (velocity[:, 0] - velocity[:, 1])
    latent_next = latent + euler_step * guided.reshape(latent.shape)
    return (received[None], refreshed[None], latent_next)


def solution(mesh):
    placed = (
        P("section", "blk", None, None),
        P("section", "blk", None, None),
        P("section", "blk", None),
        P("section", None, None, "head"),
        P("section", "head", None),
        P("section", None, "blk", None, None, "head"),
        P("section", "blk", None, None, "head"),
        P("blk"),
        P(),
        P("blk", None, None),
        P(),
        P("blk", "section", None),
    )
    return jax.shard_map(
        shards,
        mesh=mesh,
        in_specs=placed,
        out_specs=(
            P("section", "blk", None, "head"),
            P("section", None, "blk", None, "head"),
            P("blk", "section", None),
        ),
        check_vma=False,
    )
```

profile of v0, /device:TPU:0, one launch (start us, length us, event | category | flops | bytes accessed | tf_op | source)
XLA Modules:
  0.0 174.6 jit_solution(1458555649823151610)
XLA Ops:
  7.2 5.4 %all-to-all-start = ((bf16[8,64,4,2,384]{4,3,2,1,0:T(2,128)(2,1)}), bf16[8,64,4,2,384]{4,3,2,1,0:T(2,128)(2,1)}, u32[]{:S(2)}, u32[]{:S(2)}) async-start(bf16[8,64,4,2,384]{4,3,2,1,0:T(2,128)(2,1)} %bitcast.90), calls=%async_computation | async-start | bytes 6291456 | tf_op jit(solution)/shard_map/all_to_all | solution.py:84
  12.7 0.2 dynamic-slice_reduce_fusion
  12.8 0.1 broadcast_in_dim.32
  12.9 0.1 reshape.238
  13.0 0.1 dynamic_slice.19
  13.1 0.1 iota_compare_fusion.1
  13.2 0.2 tile.9
  13.5 0.3 convert_reduce_fusion
  13.8 0.5 multiply_reduce_fusion
  14.3 6.1 %copy.85 = bf16[1,1536,3,384]{1,3,2,0:T(8,128)(2,1)} copy(bf16[1,1536,3,384]{3,1,2,0:T(8,128)(2,1)} %param.15) | data formatting | bytes 7077888 | tf_op args[3]
  20.4 0.7 add_convert_fusion
  21.1 5.2 %convolution_convert_fusion = bf16[512,1152]{1,0:T(8,128)(2,1)} fusion(bf16[512,1536]{1,0:T(8,128)(2,1)S(1)} %bitcast.95, bf16[1536,1152]{0,1:T(8,128)(2,1)} %bitcast.89), kind=kOutput, calls=%fused_computation.14 | convolution fusion | flops 1812529152 | bytes 6291456 | tf_op jit(solution)/shard_map/dot_general | solution.py:71
  26.3 2.4 %copy.86 = bf16[512,1152]{0,1:T(8,128)(2,1)} copy(bf16[512,1152]{1,0:T(8,128)(2,1)} %convolution_convert_fusion) | data formatting | bytes 2359296 | tf_op jit(solution)/shard_map/convert_element_type | solution.py:75
  28.7 3.7 %reshape.237 = bf16[2,256,3,384]{1,0,3,2:T(2,128)(2,1)} reshape(bf16[512,1152]{0,1:T(8,128)(2,1)} %copy.86) | data formatting | bytes 2359296 | tf_op jit(solution)/shard_map/reshape | solution.py:76
  32.4 2.1 %fusion.35 = (bf16[2,256,1,384]{1,0,3,2:T(2,128)(2,1)S(1)}, bf16[2,256,1,384]{1,0,3,2:T(2,128)(2,1)S(1)}, bf16[2,256,1,384]{1,0,3,2:T(2,128)(2,1)S(1)}) fusion(bf16[2,256,3,384]{1,0,3,2:T(2,128)(2,1)} %reshape.237), kind=kLoop, calls=%fused_computation.71 | loop fusion | bytes 2359296 | tf_op jit(solution)/shard_map/slice | solution.py:79
  34.6 0.8 copy.89
  35.4 1.6 fusion.36
  37.0 2.0 %copy.88 = bf16[2,154,1,384]{1,3,0,2:T(8,128)(2,1)} copy(bf16[2,154,1,384]{3,2,1,0:T(2,128)(2,1)} %get-tuple-element.18) | data formatting | bytes 473088 | tf_op jit(solution)/shard_map/slice | solution.py:94
  38.9 0.8 copy.93
  39.7 2.0 %copy.92 = bf16[2,154,1,384]{1,3,0,2:T(8,128)(2,1)} copy(bf16[2,154,1,384]{3,2,1,0:T(2,128)(2,1)} %get-tuple-element.17) | data formatting | bytes 473088 | tf_op jit(solution)/shard_map/slice | solution.py:116
  41.8 0.1 iota_compare_fusion
  41.9 3.5 %fusion.9 = (f32[2,6,256]{2,1,0:T(8,128)}, f32[2,6,256,154]{2,3,1,0:T(8,128)}) fusion(pred[2,154]{1,0:T(4,128)(4,1)S(1)} %iota_compare_fusion, bf16[2,256,6,64]{1,3,2,0:T(8,128)(2,1)S(1)} %bitcast.86, bf16[2,154,6,64]{1,3,2,0:T(8,128)(2,1)} %bitcast.96), kind=kOutput, calls=%fused_computation.26 | convolution fusion | flops 61971456 | bytes 2534708 | tf_op jit(solution)/shard_map/sqhd,skhd->shqk/dot_general | solution.py:28
  45.3 2.9 %multiply_reduce_fusion.1 = (f32[2,6,256]{2,1,0:T(8,128)}, f32[2,6,256,256]{2,3,1,0:T(8,128)}) fusion(bf16[2,256,6,64]{1,3,2,0:T(8,128)(2,1)S(1)} %bitcast.87, bf16[2,256,6,64]{1,3,2,0:T(8,128)(2,1)S(1)} %bitcast.98), kind=kOutput, calls=%fused_computation.16 | convolution fusion | flops 102233088 | bytes 3944448 | tf_op jit(solution)/shard_map/sqhd,skhd->shqk/dot_general | solution.py:28
  48.2 1.6 all-to-all-done
  49.8 3.4 %copy.90 = bf16[2,4,64,4,2,384]{5,3,2,1,0,4:T(4,128)(2,1)S(1)} copy(bf16[2,4,64,4,2,384]{5,4,3,2,0,1:T(2,128)(2,1)} %bitcast.13) | data formatting | bytes 6291456 | tf_op jit(solution)/shard_map/all_to_all | solution.py:84
  53.2 2.8 %fusion.34 = (bf16[2,256,4,1,384]{4,2,1,0,3:T(4,128)(2,1)}, bf16[2,256,4,1,384]{4,2,1,0,3:T(4,128)(2,1)}) fusion(bf16[2,256,4,2,384]{4,2,1,0,3:T(4,128)(2,1)S(1)} %bitcast.83), kind=kLoop, calls=%fused_computation.70 | loop fusion | bytes 6291456 | tf_op jit(solution)/shard_map/slice | solution.py:87
  56.0 6.0 %reshape_reshape_squeeze.6 = bf16[2,1024,6,64]{3,2,1,0:T(8,128)(2,1)} reshape(bf16[2,256,4,1,384]{4,2,1,0,3:T(4,128)(2,1)} %get-tuple-element.12) | data formatting | bytes 3145728 | tf_op jit(solution)/shard_map/reshape;reshape;squeeze | solution.py:27
  62.0 4.4 %fusion = (f32[2,6,256]{2,1,0:T(8,128)S(1)}, f32[2,6,256,1024]{3,2,1,0:T(8,128)S(1)}) fusion(pred[2,1024]{1,0:T(4,128)(4,1)S(1)} %tile.9, bf16[2,256,6,64]{1,3,2,0:T(8,128)(2,1)S(1)} %bitcast.88, bf16[2,1024,6,64]{3,2,1,0:T(8,128)(2,1)} %reshape_reshape_squeeze.6), kind=kOutput, calls=%fused_computation.3 | convolution fusion | flops 412087296 | bytes 14563328 | tf_op jit(solution)/shard_map/sqhd,skhd->shqk/dot_general | solution.py:28
  66.5 3.3 %fusion.1 = f32[2,6,256]{2,1,0:T(8,128)S(1)} fusion(f32[2,6,256,1024]{3,2,1,0:T(8,128)S(1)} %get-tuple-element.24, f32[2,6,256]{2,1,0:T(8,128)S(1)} %maximum_maximum_fusion, pred[2,1024]{1,0:T(4,128)(4,1)S(1)} %tile.9), kind=kLoop, calls=%fused_computation.4 | loop fusion | flops 12579840 | bytes 12609536 | tf_op jit(solution)/shard_map/reduce_sum | solution.py:110
  69.8 2.0 %copy-done.1 = f32[2,6,256,1024]{3,2,1,0:T(8,128)} copy-done((f32[2,6,256,1024]{3,2,1,0:T(8,128)}, f32[2,6,256,1024]{3,2,1,0:T(8,128)S(1)}, u32[]{:S(2)}) %copy-start.1) | copy-done | bytes 12582936
  71.8 0.5 fusion.6
  72.3 1.0 copy-done.5
  73.4 0.5 fusion.15
  73.9 6.1 %reshape_reshape_squeeze.7 = bf16[2,1024,6,64]{3,2,1,0:T(8,128)(2,1)} reshape(bf16[2,256,4,1,384]{4,2,1,0,3:T(4,128)(2,1)} %get-tuple-element.13) | data formatting | bytes 3145728 | tf_op jit(solution)/shard_map/reshape;reshape;squeeze | solution.py:38
  80.0 2.8 %fusion.16 = f32[2,256,6,64]{1,3,2,0:T(8,128)S(1)} fusion(bf16[2,256,6,64]{1,3,2,0:T(8,128)(2,1)S(1)} %bitcast.101, f32[2,6,256,256]{2,3,1,0:T(8,128)} %get-tuple-element.28, f32[2,6,256]{2,1,0:T(8,128)S(1)} %add_add_fusion, f32[2,6,256]{2,1,0:T(8,128)S(1)} %maximum_maximum_fusion), kind=kOutput, calls=%fused_computation.33 | convolution fusion | flops 103809024 | bytes 4349952 | tf_op jit(solution)/shard_map/shqk,skhd->sqhd/dot_general | solution.py:39
  82.8 2.7 %copy-done.2 = f32[2,6,256,1024]{3,2,1,0:T(8,128)S(1)} copy-done((f32[2,6,256,1024]{3,2,1,0:T(8,128)S(1)}, f32[2,6,256,1024]{3,2,1,0:T(8,128)}, u32[]{:S(2)}) %copy-start.2) | copy-done | bytes 12582936
  85.5 5.7 %fusion.19 = f32[2,256,6,64]{1,3,2,0:T(8,128)S(1)} fusion(bf16[2,1024,6,64]{3,2,1,0:T(8,128)(2,1)} %reshape_reshape_squeeze.7, f32[2,6,256,1024]{3,2,1,0:T(8,128)S(1)} %copy-done.2, f32[2,6,256]{2,1,0:T(8,128)S(1)} %add_add_fusion, f32[2,6,256]{2,1,0:T(8,128)S(1)} %maximum_maximum_fusion, pred[2,1024]{1,0:T(4,128)(4,1)S(1)} %tile.9), kind=kOutput, calls=%fused_computation.37 | convolution fusion | flops 418381824 | bytes 14968832 | tf_op jit(solution)/shard_map/shqk,skhd->sqhd/dot_general | solution.py:39
  91.2 0.7 fusion.22
  91.9 2.2 %convolution_convert_fusion.1 = bf16[2,256,1536]{2,1,0:T(8,128)(2,1)} fusion(bf16[2,256,384]{1,2,0:T(8,128)(2,1)S(1)} %bitcast.99, bf16[1,384,1536]{2,1,0:T(8,128)(2,1)S(1)} %copy-done), kind=kOutput, calls=%fused_computation.15 | convolution fusion | flops 604766208 | bytes 3145728 | tf_op jit(solution)/shard_map/dot_general | solution.py:121
  94.1 4.9 %copy.105 = bf16[2,256,1536]{1,0,2:T(2,128)(2,1)} copy(bf16[2,256,1536]{2,1,0:T(8,128)(2,1)} %convolution_convert_fusion.1) | data formatting | bytes 3145728
  99.0 3.0 %copy.111 = bf16[192,8,2,256]{3,1,2,0:T(8,128)(2,1)} copy(bf16[192,8,2,256]{3,2,1,0:T(2,128)(2,1)} %bitcast.85) | data formatting | bytes 3145728
  102.0 0.0 reduce-scatter.4.cloned.1.call-update
  102.0 2.9 %copy.97 = bf16[2,256,2,384]{3,2,0,1:T(2,128)(2,1)} copy(bf16[2,256,2,384]{1,0,3,2:T(2,128)(2,1)S(1)} %slice-done) | data formatting | bytes 1572864 | tf_op jit(solution)/shard_map/stack | solution.py:80
  104.9 3.6 %all-to-all-start.1 = ((bf16[2,256,2,384]{3,2,0,1:T(2,128)(2,1)}), bf16[2,256,2,384]{3,2,0,1:T(2,128)(2,1)S(1)}, u32[]{:S(2)}, u32[]{:S(2)}) async-start(bf16[2,256,2,384]{3,2,0,1:T(2,128)(2,1)} %copy.97), calls=%async_computation.1 | async-start | bytes 1572864 | tf_op jit(solution)/shard_map/all_to_all | solution.py:81
  108.5 2.1 %convert_element_type.70 = f32[1,2,256,1536]{3,2,1,0:T(8,128)} convert(bf16[1,2,256,1536]{3,2,1,0:T(8,128)(2,1)S(1)} %copy-done.3) | non-fusion elementwise | flops 786432 | bytes 4718592 | tf_op jit(solution)/shard_map/convert_element_type | solution.py:65
  110.6 0.7 convert_bitcast_fusion
  111.3 27.1 %reduce-scatter.4.cloned.1.call-done = bf16[384,512]{1,0:T(8,128)(2,1)} async-done(((bf16[1536,512]{1,0:T(8,128)(2,1)}), bf16[384,512]{1,0:T(8,128)(2,1)}) %reduce-scatter.4.cloned.1.call-update) | async-done | bytes 393232
  138.4 1.1 reshape.244
  139.5 0.7 copy.106
  140.2 2.0 %fusion.28 = bf16[2,256,384]{2,1,0:T(8,128)(2,1)} fusion(bf16[2,256,384]{2,1,0:T(8,128)(2,1)S(1)} %copy.106, f32[1,2,256,1536]{3,2,1,0:T(8,128)} %convert_element_type.70, s32[]{:T(128)S(6)} %select_n.30, f32[2,384]{1,0:T(2,128)S(1)} %convert_bitcast_fusion), kind=kLoop, calls=%fused_computation.45 | loop fusion | flops 786432 | bytes 1575940 | tf_op jit(solution)/shard_map/convert_element_type | solution.py:138
  142.2 0.6 copy_bitcast_fusion
  142.8 0.1 copy.98
  142.9 0.1 copy.99
  143.0 1.7 copy.101
  144.7 1.1 dynamic-slice_select_fusion
  145.8 18.0 %all_gather.3 = bf16[2,128,1536]{2,1,0:T(8,128)(2,1)S(1)} all-gather(bf16[2,128,384]{2,1,0:T(8,128)(2,1)S(1)} %dynamic-slice_select_fusion), channel_id=1, replica_groups=mesh['section'=2,'head'=4,'blk'=4] {'head'}, dimensions={2}, use_global_device_ids=true | all-gather | bytes 983040 | tf_op jit(solution)/shard_map/all_gather | solution.py:142
  163.8 0.2 convert_reduce_fusion.1
  164.0 0.3 fusion.10
  164.4 0.4 fusion.13
  164.8 0.3 fusion.38
  165.1 0.1 reshape.240
  165.2 0.1 fusion.37
  165.3 0.6 multiply_add_fusion
  165.9 1.8 %copy.125 = bf16[1,2,256,384]{3,2,1,0:T(8,128)(2,1)} copy(bf16[1,2,256,384]{3,2,1,0:T(8,128)(2,1)} %bitcast.23) | data formatting | bytes 786432
  (57 shorter events, 0.3 us)
Async XLA Ops:
  7.2 84.8 %copy-start = (bf16[1,384,1536]{2,1,0:T(8,128)(2,1)S(1)}, bf16[1,384,1536]{2,1,0:T(8,128)(2,1)}, u32[]{:S(2)}) copy-start(bf16[1,384,1536]{2,1,0:T(8,128)(2,1)} %param.16) | copy-start | bytes 3538948
  7.2 5.5 %copy-start.18 = (s32[4,4]{1,0:T(4,128)S(1)}, s32[4,4]{1,0:T(4,128)}, u32[]{:S(2)}) copy-start(s32[4,4]{1,0:T(4,128)} %param.20) | copy-start | bytes 196
  7.2 6.2 %copy-start.17 = (bf16[1,2,2,1536]{3,2,1,0:T(2,128)(2,1)S(1)}, bf16[1,2,2,1536]{3,2,1,0:T(2,128)(2,1)}, u32[]{:S(2)}) copy-start(bf16[1,2,2,1536]{3,2,1,0:T(2,128)(2,1)} %param.13) | copy-start | bytes 36868
  7.2 6.3 %copy-start.3 = (bf16[1,2,256,1536]{3,2,1,0:T(8,128)(2,1)S(1)}, bf16[1,2,256,1536]{3,2,1,0:T(8,128)(2,1)}, u32[]{:S(2)}) copy-start(bf16[1,2,256,1536]{3,2,1,0:T(8,128)(2,1)} %param.12) | copy-start | bytes 4718596
  7.2 42.6 %all-to-all-start = ((bf16[8,64,4,2,384]{4,3,2,1,0:T(2,128)(2,1)}), bf16[8,64,4,2,384]{4,3,2,1,0:T(2,128)(2,1)}, u32[]{:S(2)}, u32[]{:S(2)}) async-start(bf16[8,64,4,2,384]{4,3,2,1,0:T(2,128)(2,1)} %bitcast.90), calls=%async_computation | async-start | bytes 6291456 | tf_op jit(solution)/shard_map/all_to_all | solution.py:84
  12.6 125.8 %reduce-scatter.4.cloned.1.call-start = ((), (), s32[]{:S(2)}) async-start(), calls=%async_computation.3 | async-start | bytes 1966080
  32.4 3.0 %copy-start.7 = (bf16[1,2,154,2,384]{4,3,2,1,0:T(2,128)(2,1)S(1)}, bf16[1,2,154,2,384]{4,3,2,1,0:T(2,128)(2,1)}, u32[]{:S(2)}) copy-start(bf16[1,2,154,2,384]{4,3,2,1,0:T(2,128)(2,1)} %param.18) | copy-start | bytes 1419268
  34.5 7.3 %copy-start.19 = (s32[2]{0:T(128)S(1)}, s32[2]{0:T(128)}, u32[]{:S(2)}) copy-start(s32[2]{0:T(128)} %param.19) | copy-start | bytes 28
  39.7 5.6 %copy-start.8 = (bf16[2,256,1,384]{1,3,0,2:T(8,128)(2,1)S(1)}, bf16[2,256,1,384]{1,3,0,2:T(8,128)(2,1)}, u32[]{:S(2)}) copy-start(bf16[2,256,1,384]{1,3,0,2:T(8,128)(2,1)} %copy.89) | copy-start | bytes 1179652
  62.0 4.5 %copy-start.12 = (f32[2,6,256]{2,1,0:T(8,128)S(1)}, f32[2,6,256]{2,1,0:T(8,128)}, u32[]{:S(2)}) copy-start(f32[2,6,256]{2,1,0:T(8,128)} %get-tuple-element.25) | copy-start | bytes 36868
  62.0 4.5 %copy-start.13 = (f32[2,6,256]{2,1,0:T(8,128)S(1)}, f32[2,6,256]{2,1,0:T(8,128)}, u32[]{:S(2)}) copy-start(f32[2,6,256]{2,1,0:T(8,128)} %get-tuple-element.27) | copy-start | bytes 36868
  66.5 5.3 %copy-start.1 = (f32[2,6,256,1024]{3,2,1,0:T(8,128)}, f32[2,6,256,1024]{3,2,1,0:T(8,128)S(1)}, u32[]{:S(2)}) copy-start(f32[2,6,256,1024]{3,2,1,0:T(8,128)S(1)} %get-tuple-element.24) | copy-start | bytes 37748740
  66.5 5.3 %copy-start.4 = (f32[2,6,256,256]{2,3,1,0:T(8,128)S(1)}, f32[2,6,256,256]{2,3,1,0:T(8,128)}, u32[]{:S(2)}) copy-start(f32[2,6,256,256]{2,3,1,0:T(8,128)} %get-tuple-element.28) | copy-start | bytes 9437188
  71.8 1.5 copy-start.5
  73.8 6.2 %copy-start.10 = (bf16[2,256,1,384]{1,3,0,2:T(8,128)(2,1)S(1)}, bf16[2,256,1,384]{1,3,0,2:T(8,128)(2,1)}, u32[]{:S(2)}) copy-start(bf16[2,256,1,384]{1,3,0,2:T(8,128)(2,1)} %copy.93) | copy-start | bytes 1179652
  80.0 5.5 %copy-start.2 = (f32[2,6,256,1024]{3,2,1,0:T(8,128)S(1)}, f32[2,6,256,1024]{3,2,1,0:T(8,128)}, u32[]{:S(2)}) copy-start(f32[2,6,256,1024]{3,2,1,0:T(8,128)} %copy-done.1) | copy-start | bytes 37748740
  85.5 5.7 %copy-start.6 = (f32[2,6,256,154]{2,3,1,0:T(8,128)S(1)}, f32[2,6,256,154]{2,3,1,0:T(8,128)}, u32[]{:S(2)}) copy-start(f32[2,6,256,154]{2,3,1,0:T(8,128)} %get-tuple-element.26) | copy-start | bytes 5677060
  85.5 5.7 %copy-start.9 = (bf16[2,154,1,384]{1,3,0,2:T(8,128)(2,1)S(1)}, bf16[2,154,1,384]{1,3,0,2:T(8,128)(2,1)}, u32[]{:S(2)}) copy-start(bf16[2,154,1,384]{1,3,0,2:T(8,128)(2,1)} %copy.92) | copy-start | bytes 709636
  99.0 3.0 %slice-start = ((bf16[2,256,3,384]{1,0,3,2:T(2,128)(2,1)}), bf16[2,256,2,384]{1,0,3,2:T(2,128)(2,1)S(1)}, s32[]{:S(2)}) async-start(bf16[2,256,3,384]{1,0,3,2:T(2,128)(2,1)} %reshape.237), calls=%async_computation.4 | async-start | bytes 1572864 | tf_op jit(solution)/shard_map/stack | solution.py:80
  104.9 5.7 %copy-start.15 = (bf16[2,2,1536]{2,1,0:T(2,128)(2,1)S(1)}, bf16[2,2,1536]{2,1,0:T(2,128)(2,1)}, u32[]{:S(2)}) copy-start(bf16[2,2,1536]{2,1,0:T(2,128)(2,1)} %param.21) | copy-start | bytes 36868
  104.9 37.9 %all-to-all-start.1 = ((bf16[2,256,2,384]{3,2,0,1:T(2,128)(2,1)}), bf16[2,256,2,384]{3,2,0,1:T(2,128)(2,1)S(1)}, u32[]{:S(2)}, u32[]{:S(2)}) async-start(bf16[2,256,2,384]{3,2,0,1:T(2,128)(2,1)} %copy.97), calls=%async_computation.1 | async-start | bytes 1572864 | tf_op jit(solution)/shard_map/all_to_all | solution.py:81
  142.2 2.5 %collective-permute-start = (bf16[2,256,384]{2,1,0:T(8,128)(2,1)}, bf16[2,256,384]{2,1,0:T(8,128)(2,1)}, u32[]{:S(2)}, u32[]{:S(2)}) collective-permute-start(bf16[2,256,384]{2,1,0:T(8,128)(2,1)} %fusion.28), channel_id=1, source_target_pairs={{0,16},{16,0},{1,17},{17,1},{2,18},{18,2},{3,19},{19,3},{4,20},{20... | collective-permute-start | bytes 1179656 | tf_op jit(solution)/shard_map/ppermute | solution.py:14
  142.9 21.5 %copy-start.14 = (f32[2,1536]{1,0:T(2,128)S(1)}, f32[2,1536]{1,0:T(2,128)}, u32[]{:S(2)}) copy-start(f32[2,1536]{1,0:T(2,128)} %get-tuple-element.32) | copy-start | bytes 36868
  143.0 21.7 %copy-start.11 = (bf16[1536,64]{0,1:T(8,128)(2,1)S(1)}, bf16[1536,64]{0,1:T(8,128)(2,1)}, u32[]{:S(2)}) copy-start(bf16[1536,64]{0,1:T(8,128)(2,1)} %param.22) | copy-start | bytes 589828
  144.7 20.6 %copy-start.16 = (f32[1,64,128]{2,1,0:T(8,128)S(1)}, f32[1,64,128]{2,1,0:T(8,128)}, u32[]{:S(2)}) copy-start(f32[1,64,128]{2,1,0:T(8,128)} %param.23) | copy-start | bytes 98308
Sparse Core Ops, SparseCore 0:
  102.1 36.2 reduce-scatter.3
where the time goes:
time: 176 us; the launch traced here: 175 us
  local copies, waits for them, and re-layouts  63.3 us (36%)
  waiting for transfers between devices  28.7 us (16%)
  matrix products  27.7 us (16%)
  blocking collectives  18 us (10%)
  between operations  14.4 us (8%)
  other arithmetic  13.4 us (8%)
  starting transfers between devices  9.07 us (5%)
    unnamed x2, waiting for transfers between devices  27.1 us
    unnamed x49, local copies, waits for them, and re-layouts  25.6 us
    all_gather x1, blocking collectives, shards(): final_rows = lax.all_gather(last_half, 'head', axis=2, tiled=True)  18 us
    dot_general x3, matrix products, piece_scores(): jnp.einsum('sqhd,skhd->shqk', query_heads, key_heads, preferred_element_t...  10.8 us
    dot_general x3, matrix products, piece_values(): jnp.einsum('shqk,skhd->sqhd', probs_piece, value_heads, preferred_element...  9.17 us
    another operation x1, local copies, waits for them, and re-layouts, piece_values(): value_heads = value_piece.reshape(seq_dev, -1, head_count, HEAD_DIM)  6.13 us
    another operation x1, local copies, waits for them, and re-layouts, piece_scores(): key_heads = key_piece.reshape(seq_dev, -1, head_count, HEAD_DIM)  6.03 us
    all_to_all x1, starting transfers between devices, shards(): lax.all_to_all(local_cache, 'blk', split_axis=0, concat_axis=1, tiled=True)  5.44 us
  transfers between devices with their start and end apart: 4, of which 2 were waited for; matrix products, arithmetic and copies ran while one was open for 27% of the time, Pallas kernels for 0%

commit v1 on v0

--- a/solution.py
+++ b/solution.py
@@ -7,6 +7,20 @@
 norm_eps = 1e-06
 guidance = 4.0
 euler_step = -0.25
+
+
+def spread_the_pairs_all(state, k_dim, work_x):
+    value_now = state.shape
+    block_now = state.reshape(
+        *value_now[:k_dim], work_x, value_now[k_dim] // work_x, *value_now[k_dim + 1 :]
+    )
+    return jnp.moveaxis(block_now, k_dim, 0)
+
+
+def record_state(point, array_dim):
+    w2 = list(point.shape[1:])
+    w2[array_dim] *= point.shape[0]
+    return jnp.moveaxis(point, 0, array_dim).reshape(w2)
 
 
 def passed_along(shard, axis, by):
@@ -81,7 +95,17 @@
     refreshed = lax.all_to_all(fresh_kv, "blk", split_axis=1, concat_axis=0, tiled=True)
     local_cache = kv_cache[0]
     patch_count = local_cache.shape[2]
-    fetched = lax.all_to_all(local_cache, "blk", split_axis=0, concat_axis=1, tiled=True)
+    block_last = lax.axis_size("blk")
+    all_values = lax.axis_index("blk")
+    kept_arr, long_array = (block_last, all_values)
+    v_now = spread_the_pairs_all(local_cache, 0, kept_arr)
+    grid = [v_now[long_array]]
+    for dev in range(1, kept_arr):
+        x_next = v_now[long_array ^ dev]
+        taken_in = lax.ppermute(x_next, "blk", [(at, at ^ dev) for at in range(kept_arr)])
+        grid.append(taken_in)
+    v_now = jnp.stack(grid)[long_array ^ jnp.arange(kept_arr)]
+    fetched = record_state(v_now, 1)
     keep_patch = jnp.arange(patch_count, dtype=jnp.int32)[None, :] != own_patch[:, None]
     stale_counted = jnp.tile(keep_patch, (1, patch_rows))
     stale_keys = fetched[:, :, :, 0].reshape(seq_dev, -1, group_width)

time: 176 us -> 194 us (1.10)
  local copies, waits for them, and re-layouts: 63.3 us -> 76.3 us
  other arithmetic: 13.4 us -> 19.7 us
    gather x0 -> x1, local copies, waits for them, and re-layouts: none -> 10.5 us  [shards(): v_now = jnp.stack(grid)[long_array ^ jnp.arange(kept_arr)]]
    another operation x1 -> x2, other arithmetic: 0.69 us -> 8.91 us  [the longest x1 8.22 us: shards(): v_now = jnp.stack(grid)[long_array ^ jnp.arange(kept_arr)]]
    all_to_all x1 -> x0, starting transfers between devices: 5.44 us -> none  [shards(): lax.all_to_all(local_cache, 'blk', split_axis=0, concat_axis=1, tiled=True)]
    dynamic_slice x0 -> x1, local copies, waits for them, and re-layouts: none -> 4.71 us  [shards(): grid = [v_now[long_array]]]
    ppermute x0 -> x3, starting transfers between devices: none -> 4.47 us  [shards(): lax.ppermute(x_next, 'blk', [(at, at ^ dev) for at in range(kept_arr)])]
    all_to_all x1 -> x0, local copies, waits for them, and re-layouts: 3.4 us -> none  [shards(): lax.all_to_all(local_cache, 'blk', split_axis=0, concat_axis=1, tiled=True)]
    transpose x0 -> x1, local copies, waits for them, and re-layouts: none -> 3.4 us  [record_state(): return jnp.moveaxis(point, 0, array_dim).reshape(w2)]
    unnamed x49, local copies, waits for them, and re-layouts: 25.6 us -> 23.4 us
  transfers between devices with their start and end apart: 4 -> 6, of which waited for: 2 -> 1; matrix products, arithmetic and copies ran while one was open for 27% -> 24% of each run, Pallas kernels for 0% -> 0%
where the time goes in v1:
time: 194 us; the launch traced here: 192 us
  local copies, waits for them, and re-layouts  76.3 us (39%)
  matrix products  27.9 us (14%)
  waiting for transfers between devices  27.1 us (14%)
  other arithmetic  19.7 us (10%)
  blocking collectives  18 us (9%)
  between operations  14.5 us (7%)
  starting transfers between devices  8.9 us (5%)
    unnamed x2, waiting for transfers between devices  27.1 us
    unnamed x49, local copies, waits for them, and re-layouts  23.4 us
    all_gather x1, blocking collectives, shards(): final_rows = lax.all_gather(last_half, 'head', axis=2, tiled=True)  18 us
    dot_general x3, matrix products, piece_scores(): jnp.einsum('sqhd,skhd->shqk', query_heads, key_heads, preferred_element_t...  11 us
    gather x1, local copies, waits for them, and re-layouts, shards(): v_now = jnp.stack(grid)[long_array ^ jnp.arange(kept_arr)]  10.5 us
    dot_general x3, matrix products, piece_values(): jnp.einsum('shqk,skhd->sqhd', probs_piece, value_heads, preferred_element...  9.16 us
    another operation x1, other arithmetic, shards(): v_now = jnp.stack(grid)[long_array ^ jnp.arange(kept_arr)]  8.22 us
    another operation x1, local copies, waits for them, and re-layouts, piece_values(): value_heads = value_piece.reshape(seq_dev, -1, head_count, HEAD_DIM)  6.16 us
  transfers between devices with their start and end apart: 6, of which 1 were waited for; matrix products, arithmetic and copies ran while one was open for 24% of the time, Pallas kernels for 0%

profile of v1, /device:TPU:0, one launch (start us, length us, event | category | flops | bytes accessed | tf_op | source)
XLA Modules:
  0.0 192.4 jit_solution(14317392326401064994)
XLA Ops:
  7.3 4.7 %constant_dynamic-slice_fusion = (bf16[1,2,64,4,2,384]{5,4,3,2,1,0:T(2,128)(2,1)}, bf16[2,64,4,2,384]{4,3,2,1,0:T(2,128)(2,1)}, bf16[2,64,4,2,384]{4,3,2,1,0:T(2,128)(2,1)}, bf16[2,64,4,2,384]{4,3,2,1,0:T(2,128)(2,1)}) fusion(bf16[4,2,64,4,2,384]{5,4,3,2,1,0:T(2,128)(2,1)} %bitcast.100, s32[]{:T(128)S(6)} %select_n.56, s32[]{:T(128)S(6)} %select_n.59, ...), kind=kLoop, calls=%fused_computation.65 | loop fusion | bytes 6291472 | tf_op jit(solution)/shard_map/dynamic_slice | solution.py:102
  12.0 2.9 %collective-permute-start = (bf16[2,64,4,2,384]{4,3,2,1,0:T(2,128)(2,1)}, bf16[2,64,4,2,384]{4,3,2,1,0:T(2,128)(2,1)}, u32[]{:S(2)}, u32[]{:S(2)}) collective-permute-start(bf16[2,64,4,2,384]{4,3,2,1,0:T(2,128)(2,1)} %get-tuple-element.17), channel_id=1, source_target_pairs={{0,1},{1,0},{2,3},{3,2},{4,5},{5,4},{6,7},{7,6},{8,9},{9,8},{10,11... | collective-permute-start | bytes 2359304 | tf_op jit(solution)/shard_map/ppermute | solution.py:105
  14.9 1.5 collective-permute-start.1
  16.5 0.2 fusion.29
  16.7 0.1 broadcast_in_dim.32
  16.7 0.1 reshape.257
  16.8 0.1 dynamic_slice.31
  16.9 0.1 iota_compare_fusion.1
  17.0 0.2 tile.9
  17.3 0.3 convert_reduce_fusion
  17.6 0.5 multiply_reduce_fusion
  18.1 6.1 %copy.85 = bf16[1,1536,3,384]{1,3,2,0:T(8,128)(2,1)} copy(bf16[1,1536,3,384]{3,1,2,0:T(8,128)(2,1)} %param.15) | data formatting | bytes 7077888 | tf_op args[3]
  24.3 0.7 add_convert_fusion
  24.9 5.3 %convolution_convert_fusion = bf16[512,1152]{1,0:T(8,128)(2,1)} fusion(bf16[512,1536]{1,0:T(8,128)(2,1)S(1)} %bitcast.105, bf16[1536,1152]{0,1:T(8,128)(2,1)} %bitcast.99), kind=kOutput, calls=%fused_computation.16 | convolution fusion | flops 1812529152 | bytes 6291456 | tf_op jit(solution)/shard_map/dot_general | solution.py:85
  30.2 2.4 %copy.86 = bf16[512,1152]{0,1:T(8,128)(2,1)} copy(bf16[512,1152]{1,0:T(8,128)(2,1)} %convolution_convert_fusion) | data formatting | bytes 2359296 | tf_op jit(solution)/shard_map/convert_element_type | solution.py:89
  32.6 3.7 %reshape.256 = bf16[2,256,3,384]{1,0,3,2:T(2,128)(2,1)} reshape(bf16[512,1152]{0,1:T(8,128)(2,1)} %copy.86) | data formatting | bytes 2359296 | tf_op jit(solution)/shard_map/reshape | solution.py:90
  36.3 2.1 %fusion.37 = (bf16[2,256,1,384]{1,0,3,2:T(2,128)(2,1)S(1)}, bf16[2,256,1,384]{1,0,3,2:T(2,128)(2,1)S(1)}, bf16[2,256,1,384]{1,0,3,2:T(2,128)(2,1)S(1)}) fusion(bf16[2,256,3,384]{1,0,3,2:T(2,128)(2,1)} %reshape.256), kind=kLoop, calls=%fused_computation.82 | loop fusion | bytes 2359296 | tf_op jit(solution)/shard_map/slice | solution.py:93
  38.5 0.8 copy.89
  39.3 1.6 fusion.38
  40.9 2.0 %copy.88 = bf16[2,154,1,384]{1,3,0,2:T(8,128)(2,1)} copy(bf16[2,154,1,384]{3,2,1,0:T(2,128)(2,1)} %get-tuple-element.22) | data formatting | bytes 473088 | tf_op jit(solution)/shard_map/slice | solution.py:118
  42.9 0.8 copy.93
  43.7 2.0 %copy.92 = bf16[2,154,1,384]{1,3,0,2:T(8,128)(2,1)} copy(bf16[2,154,1,384]{3,2,1,0:T(2,128)(2,1)} %get-tuple-element.21) | data formatting | bytes 473088 | tf_op jit(solution)/shard_map/slice | solution.py:140
  45.7 0.1 iota_compare_fusion
  45.8 3.5 %fusion.9 = (f32[2,6,256]{2,1,0:T(8,128)}, f32[2,6,256,154]{2,3,1,0:T(8,128)}) fusion(pred[2,154]{1,0:T(4,128)(4,1)S(1)} %iota_compare_fusion, bf16[2,256,6,64]{1,3,2,0:T(8,128)(2,1)S(1)} %bitcast.96, bf16[2,154,6,64]{1,3,2,0:T(8,128)(2,1)} %bitcast.106), kind=kOutput, calls=%fused_computation.28 | convolution fusion | flops 61971456 | bytes 2534708 | tf_op jit(solution)/shard_map/sqhd,skhd->shqk/dot_general | solution.py:42
  49.4 2.9 %multiply_reduce_fusion.1 = (f32[2,6,256]{2,1,0:T(8,128)}, f32[2,6,256,256]{2,3,1,0:T(8,128)}) fusion(bf16[2,256,6,64]{1,3,2,0:T(8,128)(2,1)S(1)} %bitcast.97, bf16[2,256,6,64]{1,3,2,0:T(8,128)(2,1)S(1)} %bitcast.108), kind=kOutput, calls=%fused_computation.18 | convolution fusion | flops 102233088 | bytes 3944448 | tf_op jit(solution)/shard_map/sqhd,skhd->shqk/dot_general | solution.py:42
  52.3 8.2 %pad_maximum_fusion = bf16[4,2,64,4,2,384]{5,4,3,2,1,0:T(2,128)(2,1)} fusion(bf16[1,2,64,4,2,384]{5,4,3,2,1,0:T(2,128)(2,1)} %bitcast.17, bf16[1,2,64,4,2,384]{5,4,3,2,1,0:T(2,128)(2,1)} %bitcast.15, bf16[1,2,64,4,2,384]{5,4,3,2,1,0:T(2,128)(2,1)} %bitcast.13, bf16[1,2,64,4,2,384]{5,4,3,2,1,0:T(2,128)(2,1)S(1)} %copy-done.7), kind=kLoop, calls=%fused_computation.7 | loop fusion | flops 4718592 | bytes 6291456 | tf_op jit(solution)/shard_map/stack | solution.py:107
  60.5 10.5 %gather_fusion = bf16[4,2,64,4,2,384]{5,4,3,2,1,0:T(2,128)(2,1)} fusion(bf16[4,2,64,4,2,384]{5,4,3,2,1,0:T(2,128)(2,1)} %pad_maximum_fusion, s32[1024]{0:T(1024)S(1)} %pad_clamp_fusion), kind=kCustom, calls=%fused_computation | custom fusion | bytes 6291472 | tf_op jit(solution)/shard_map/gather | solution.py:107
  71.0 3.4 %copy.90 = bf16[2,4,64,4,2,384]{5,3,2,1,0,4:T(4,128)(2,1)S(1)} copy(bf16[2,4,64,4,2,384]{5,4,3,2,0,1:T(2,128)(2,1)} %bitcast.93) | data formatting | bytes 6291456 | tf_op jit(solution)/shard_map/transpose | solution.py:23
  74.4 2.7 %fusion.36 = (bf16[2,256,4,1,384]{4,2,1,0,3:T(4,128)(2,1)}, bf16[2,256,4,1,384]{4,2,1,0,3:T(4,128)(2,1)}) fusion(bf16[2,256,4,2,384]{4,2,1,0,3:T(4,128)(2,1)S(1)} %bitcast.92), kind=kLoop, calls=%fused_computation.81 | loop fusion | bytes 6291456 | tf_op jit(solution)/shard_map/slice | solution.py:112
  77.1 6.0 %reshape_reshape_squeeze.6 = bf16[2,1024,6,64]{3,2,1,0:T(8,128)(2,1)} reshape(bf16[2,256,4,1,384]{4,2,1,0,3:T(4,128)(2,1)} %get-tuple-element.13) | data formatting | bytes 3145728 | tf_op jit(solution)/shard_map/reshape;reshape;squeeze | solution.py:41
  83.1 4.6 %fusion = (f32[2,6,256]{2,1,0:T(8,128)S(1)}, f32[2,6,256,1024]{3,2,1,0:T(8,128)S(1)}) fusion(pred[2,1024]{1,0:T(4,128)(4,1)S(1)} %tile.9, bf16[2,256,6,64]{1,3,2,0:T(8,128)(2,1)S(1)} %bitcast.98, bf16[2,1024,6,64]{3,2,1,0:T(8,128)(2,1)} %reshape_reshape_squeeze.6), kind=kOutput, calls=%fused_computation.4 | convolution fusion | flops 412087296 | bytes 14563328 | tf_op jit(solution)/shard_map/sqhd,skhd->shqk/dot_general | solution.py:42
  87.8 0.5 fusion.6
  88.3 2.4 %copy-done.5 = f32[2,6,256,154]{2,3,1,0:T(8,128)S(1)} copy-done((f32[2,6,256,154]{2,3,1,0:T(8,128)S(1)}, f32[2,6,256,154]{2,3,1,0:T(8,128)}, u32[]{:S(2)}) %copy-start.5) | copy-done | bytes 1892376
  90.7 0.5 fusion.15
  91.2 3.1 %fusion.1 = f32[2,6,256]{2,1,0:T(8,128)S(1)} fusion(f32[2,6,256,1024]{3,2,1,0:T(8,128)S(1)} %get-tuple-element.28, f32[2,6,256]{2,1,0:T(8,128)S(1)} %maximum_maximum_fusion, pred[2,1024]{1,0:T(4,128)(4,1)S(1)} %tile.9), kind=kLoop, calls=%fused_computation.5 | loop fusion | flops 12579840 | bytes 12609536 | tf_op jit(solution)/shard_map/reduce_sum | solution.py:134
  94.3 6.2 %reshape_reshape_squeeze.7 = bf16[2,1024,6,64]{3,2,1,0:T(8,128)(2,1)} reshape(bf16[2,256,4,1,384]{4,2,1,0,3:T(4,128)(2,1)} %get-tuple-element.12) | data formatting | bytes 3145728 | tf_op jit(solution)/shard_map/reshape;reshape;squeeze | solution.py:52
  100.5 2.8 %fusion.16 = f32[2,256,6,64]{1,3,2,0:T(8,128)S(1)} fusion(bf16[2,256,6,64]{1,3,2,0:T(8,128)(2,1)S(1)} %bitcast.112, f32[2,6,256,256]{2,3,1,0:T(8,128)} %get-tuple-element.32, f32[2,6,256]{2,1,0:T(8,128)S(1)} %add_add_fusion, f32[2,6,256]{2,1,0:T(8,128)S(1)} %maximum_maximum_fusion), kind=kOutput, calls=%fused_computation.35 | convolution fusion | flops 103809024 | bytes 4349952 | tf_op jit(solution)/shard_map/shqk,skhd->sqhd/dot_general | solution.py:53
  103.3 2.7 %copy-done.2 = f32[2,6,256,1024]{3,2,1,0:T(8,128)S(1)} copy-done((f32[2,6,256,1024]{3,2,1,0:T(8,128)S(1)}, f32[2,6,256,1024]{3,2,1,0:T(8,128)}, u32[]{:S(2)}) %copy-start.2) | copy-done | bytes 12582936
  106.0 5.7 %fusion.19 = f32[2,256,6,64]{1,3,2,0:T(8,128)S(1)} fusion(f32[2,6,256,1024]{3,2,1,0:T(8,128)S(1)} %copy-done.2, f32[2,6,256]{2,1,0:T(8,128)S(1)} %add_add_fusion, f32[2,6,256]{2,1,0:T(8,128)S(1)} %maximum_maximum_fusion, pred[2,1024]{1,0:T(4,128)(4,1)S(1)} %tile.9, bf16[2,1024,6,64]{3,2,1,0:T(8,128)(2,1)} %reshape_reshape_squeeze.7), kind=kOutput, calls=%fused_computation.39 | convolution fusion | flops 418381824 | bytes 14968832 | tf_op jit(solution)/shard_map/shqk,skhd->sqhd/dot_general | solution.py:53
  111.7 0.7 fusion.22
  112.4 2.2 %convolution_convert_fusion.1 = bf16[2,256,1536]{2,1,0:T(8,128)(2,1)} fusion(bf16[2,256,384]{1,2,0:T(8,128)(2,1)S(1)} %bitcast.110, bf16[1,384,1536]{2,1,0:T(8,128)(2,1)S(1)} %copy-done), kind=kOutput, calls=%fused_computation.17 | convolution fusion | flops 604766208 | bytes 3145728 | tf_op jit(solution)/shard_map/dot_general | solution.py:145
  114.6 4.9 %copy.105 = bf16[2,256,1536]{1,0,2:T(2,128)(2,1)} copy(bf16[2,256,1536]{2,1,0:T(8,128)(2,1)} %convolution_convert_fusion.1) | data formatting | bytes 3145728
  119.5 3.0 %copy.111 = bf16[192,8,2,256]{3,1,2,0:T(8,128)(2,1)} copy(bf16[192,8,2,256]{3,2,1,0:T(2,128)(2,1)} %bitcast.95) | data formatting | bytes 3145728
  122.5 2.9 %copy.97 = bf16[2,256,2,384]{3,2,0,1:T(2,128)(2,1)} copy(bf16[2,256,2,384]{1,0,3,2:T(2,128)(2,1)S(1)} %slice-done) | data formatting | bytes 1572864 | tf_op jit(solution)/shard_map/stack | solution.py:94
  125.4 4.3 %all-to-all-start = ((bf16[2,256,2,384]{3,2,0,1:T(2,128)(2,1)}), bf16[2,256,2,384]{3,2,0,1:T(2,128)(2,1)S(1)}, u32[]{:S(2)}, u32[]{:S(2)}) async-start(bf16[2,256,2,384]{3,2,0,1:T(2,128)(2,1)} %copy.97), calls=%async_computation | async-start | bytes 1572864 | tf_op jit(solution)/shard_map/all_to_all | solution.py:95
  129.7 2.1 %convert_element_type.70 = f32[1,2,256,1536]{3,2,1,0:T(8,128)} convert(bf16[1,2,256,1536]{3,2,1,0:T(8,128)(2,1)S(1)} %copy-done.3) | non-fusion elementwise | flops 786432 | bytes 4718592 | tf_op jit(solution)/shard_map/convert_element_type | solution.py:79
  131.8 0.7 convert_bitcast_fusion
  132.5 27.1 %reduce-scatter.4.cloned.1.call-done = bf16[384,512]{1,0:T(8,128)(2,1)} async-done(((bf16[1536,512]{1,0:T(8,128)(2,1)}), bf16[384,512]{1,0:T(8,128)(2,1)}) %reduce-scatter.4.cloned.1.call-update) | async-done | bytes 393232
  159.6 1.1 reshape.272
  160.7 0.7 copy.106
  161.4 1.2 fusion.28
  162.7 0.1 collective-permute-start.3
  162.8 0.1 copy.98
  162.9 0.1 copy.99
  163.0 1.7 copy.101
  164.7 18.0 %all_gather.3 = bf16[2,128,1536]{2,1,0:T(8,128)(2,1)S(1)} all-gather(bf16[2,128,384]{2,1,0:T(8,128)(2,1)S(1)} %dynamic-slice_select_fusion), channel_id=1, replica_groups=mesh['section'=2,'head'=4,'blk'=4] {'head'}, dimensions={2}, use_global_device_ids=true | all-gather | bytes 983040 | tf_op jit(solution)/shard_map/all_gather | solution.py:166
  182.7 0.2 convert_reduce_fusion.1
  182.9 0.3 fusion.10
  183.3 0.4 fusion.13
  183.7 0.3 fusion.40
  184.0 0.1 reshape.260
  184.2 0.1 fusion.39
  184.2 0.6 multiply_add_fusion
  184.9 0.7 copy.125
  (66 shorter events, 0.4 us)
Async XLA Ops:
  7.2 105.3 %copy-start = (bf16[1,384,1536]{2,1,0:T(8,128)(2,1)S(1)}, bf16[1,384,1536]{2,1,0:T(8,128)(2,1)}, u32[]{:S(2)}) copy-start(bf16[1,384,1536]{2,1,0:T(8,128)(2,1)} %param.16) | copy-start | bytes 3538948
  7.2 152.5 %reduce-scatter.4.cloned.1.call-start = ((), (), s32[]{:S(2)}) async-start(), calls=%async_computation.2 | async-start | bytes 1966080
  7.2 9.2 %copy-start.18 = (s32[4,4]{1,0:T(4,128)S(1)}, s32[4,4]{1,0:T(4,128)}, u32[]{:S(2)}) copy-start(s32[4,4]{1,0:T(4,128)} %param.20) | copy-start | bytes 196
  7.3 10.0 %copy-start.17 = (bf16[1,2,2,1536]{3,2,1,0:T(2,128)(2,1)S(1)}, bf16[1,2,2,1536]{3,2,1,0:T(2,128)(2,1)}, u32[]{:S(2)}) copy-start(bf16[1,2,2,1536]{3,2,1,0:T(2,128)(2,1)} %param.13) | copy-start | bytes 36868
  7.3 10.0 %copy-start.3 = (bf16[1,2,256,1536]{3,2,1,0:T(8,128)(2,1)S(1)}, bf16[1,2,256,1536]{3,2,1,0:T(8,128)(2,1)}, u32[]{:S(2)}) copy-start(bf16[1,2,256,1536]{3,2,1,0:T(8,128)(2,1)} %param.12) | copy-start | bytes 4718596
  12.0 40.2 %collective-permute-start = (bf16[2,64,4,2,384]{4,3,2,1,0:T(2,128)(2,1)}, bf16[2,64,4,2,384]{4,3,2,1,0:T(2,128)(2,1)}, u32[]{:S(2)}, u32[]{:S(2)}) collective-permute-start(bf16[2,64,4,2,384]{4,3,2,1,0:T(2,128)(2,1)} %get-tuple-element.17), channel_id=1, source_target_pairs={{0,1},{1,0},{2,3},{3,2},{4,5},{5,4},{6,7},{7,6},{8,9},{9,8},{10,11... | collective-permute-start | bytes 2359304 | tf_op jit(solution)/shard_map/ppermute | solution.py:105
  14.9 37.3 %collective-permute-start.1 = (bf16[2,64,4,2,384]{4,3,2,1,0:T(2,128)(2,1)}, bf16[2,64,4,2,384]{4,3,2,1,0:T(2,128)(2,1)}, u32[]{:S(2)}, u32[]{:S(2)}) collective-permute-start(bf16[2,64,4,2,384]{4,3,2,1,0:T(2,128)(2,1)} %get-tuple-element.16), channel_id=1, source_target_pairs={{0,2},{1,3},{2,0},{3,1},{4,6},{5,7},{6,4},{7,5},{8,10},{9,11},{10,... | collective-permute-start | bytes 2359304 | tf_op jit(solution)/shard_map/ppermute | solution.py:105
  16.4 35.8 %collective-permute-start.2 = (bf16[2,64,4,2,384]{4,3,2,1,0:T(2,128)(2,1)}, bf16[2,64,4,2,384]{4,3,2,1,0:T(2,128)(2,1)}, u32[]{:S(2)}, u32[]{:S(2)}) collective-permute-start(bf16[2,64,4,2,384]{4,3,2,1,0:T(2,128)(2,1)} %get-tuple-element.15), channel_id=1, source_target_pairs={{0,3},{1,2},{2,1},{3,0},{4,7},{5,6},{6,5},{7,4},{8,11},{9,10},{10,... | collective-permute-start | bytes 2359304 | tf_op jit(solution)/shard_map/ppermute | solution.py:105
  36.3 3.0 %copy-start.8 = (bf16[1,2,154,2,384]{4,3,2,1,0:T(2,128)(2,1)S(1)}, bf16[1,2,154,2,384]{4,3,2,1,0:T(2,128)(2,1)}, u32[]{:S(2)}) copy-start(bf16[1,2,154,2,384]{4,3,2,1,0:T(2,128)(2,1)} %param.18) | copy-start | bytes 1419268
  38.4 7.3 %copy-start.19 = (s32[2]{0:T(128)S(1)}, s32[2]{0:T(128)}, u32[]{:S(2)}) copy-start(s32[2]{0:T(128)} %param.19) | copy-start | bytes 28
  43.7 5.7 %copy-start.9 = (bf16[2,256,1,384]{1,3,0,2:T(8,128)(2,1)S(1)}, bf16[2,256,1,384]{1,3,0,2:T(8,128)(2,1)}, u32[]{:S(2)}) copy-start(bf16[2,256,1,384]{1,3,0,2:T(8,128)(2,1)} %copy.89) | copy-start | bytes 1179652
  45.8 6.4 %copy-start.7 = (bf16[1,2,64,4,2,384]{5,4,3,2,1,0:T(2,128)(2,1)S(1)}, bf16[1,2,64,4,2,384]{5,4,3,2,1,0:T(2,128)(2,1)}, u32[]{:S(2)}) copy-start(bf16[1,2,64,4,2,384]{5,4,3,2,1,0:T(2,128)(2,1)} %get-tuple-element.14) | copy-start | bytes 2359300
  83.1 4.6 %copy-start.13 = (f32[2,6,256]{2,1,0:T(8,128)S(1)}, f32[2,6,256]{2,1,0:T(8,128)}, u32[]{:S(2)}) copy-start(f32[2,6,256]{2,1,0:T(8,128)} %get-tuple-element.29) | copy-start | bytes 36868
  83.1 4.6 %copy-start.14 = (f32[2,6,256]{2,1,0:T(8,128)S(1)}, f32[2,6,256]{2,1,0:T(8,128)}, u32[]{:S(2)}) copy-start(f32[2,6,256]{2,1,0:T(8,128)} %get-tuple-element.31) | copy-start | bytes 36868
  83.1 4.6 %copy-start.4 = (f32[2,6,256,256]{2,3,1,0:T(8,128)S(1)}, f32[2,6,256,256]{2,3,1,0:T(8,128)}, u32[]{:S(2)}) copy-start(f32[2,6,256,256]{2,3,1,0:T(8,128)} %get-tuple-element.32) | copy-start | bytes 9437188
  87.7 6.6 %copy-start.1 = (f32[2,6,256,1024]{3,2,1,0:T(8,128)}, f32[2,6,256,1024]{3,2,1,0:T(8,128)S(1)}, u32[]{:S(2)}) copy-start(f32[2,6,256,1024]{3,2,1,0:T(8,128)S(1)} %get-tuple-element.28) | copy-start | bytes 37748740
  87.7 3.0 %copy-start.5 = (f32[2,6,256,154]{2,3,1,0:T(8,128)S(1)}, f32[2,6,256,154]{2,3,1,0:T(8,128)}, u32[]{:S(2)}) copy-start(f32[2,6,256,154]{2,3,1,0:T(8,128)} %get-tuple-element.30) | copy-start | bytes 5677060
  94.3 6.2 %copy-start.11 = (bf16[2,256,1,384]{1,3,0,2:T(8,128)(2,1)S(1)}, bf16[2,256,1,384]{1,3,0,2:T(8,128)(2,1)}, u32[]{:S(2)}) copy-start(bf16[2,256,1,384]{1,3,0,2:T(8,128)(2,1)} %copy.93) | copy-start | bytes 1179652
  100.5 5.5 %copy-start.2 = (f32[2,6,256,1024]{3,2,1,0:T(8,128)S(1)}, f32[2,6,256,1024]{3,2,1,0:T(8,128)}, u32[]{:S(2)}) copy-start(f32[2,6,256,1024]{3,2,1,0:T(8,128)} %copy-done.1) | copy-start | bytes 37748740
  106.0 5.7 %copy-start.6 = (f32[2,6,256,154]{2,3,1,0:T(8,128)S(1)}, f32[2,6,256,154]{2,3,1,0:T(8,128)}, u32[]{:S(2)}) copy-start(f32[2,6,256,154]{2,3,1,0:T(8,128)} %get-tuple-element.30) | copy-start | bytes 5677060
  106.0 5.7 %copy-start.10 = (bf16[2,154,1,384]{1,3,0,2:T(8,128)(2,1)S(1)}, bf16[2,154,1,384]{1,3,0,2:T(8,128)(2,1)}, u32[]{:S(2)}) copy-start(bf16[2,154,1,384]{1,3,0,2:T(8,128)(2,1)} %copy.92) | copy-start | bytes 709636
  119.5 3.0 %slice-start = ((bf16[2,256,3,384]{1,0,3,2:T(2,128)(2,1)}), bf16[2,256,2,384]{1,0,3,2:T(2,128)(2,1)S(1)}, s32[]{:S(2)}) async-start(bf16[2,256,3,384]{1,0,3,2:T(2,128)(2,1)} %reshape.256), calls=%async_computation.3 | async-start | bytes 1572864 | tf_op jit(solution)/shard_map/stack | solution.py:94
  125.4 6.4 %copy-start.15 = (bf16[2,2,1536]{2,1,0:T(2,128)(2,1)S(1)}, bf16[2,2,1536]{2,1,0:T(2,128)(2,1)}, u32[]{:S(2)}) copy-start(bf16[2,2,1536]{2,1,0:T(2,128)(2,1)} %param.21) | copy-start | bytes 36868
  125.4 37.4 %all-to-all-start = ((bf16[2,256,2,384]{3,2,0,1:T(2,128)(2,1)}), bf16[2,256,2,384]{3,2,0,1:T(2,128)(2,1)S(1)}, u32[]{:S(2)}, u32[]{:S(2)}) async-start(bf16[2,256,2,384]{3,2,0,1:T(2,128)(2,1)} %copy.97), calls=%async_computation | async-start | bytes 1572864 | tf_op jit(solution)/shard_map/all_to_all | solution.py:95
  162.7 2.0 %collective-permute-start.3 = (bf16[2,256,384]{2,1,0:T(8,128)(2,1)S(1)}, bf16[2,256,384]{2,1,0:T(8,128)(2,1)S(1)}, u32[]{:S(2)}, u32[]{:S(2)}) collective-permute-start(bf16[2,256,384]{2,1,0:T(8,128)(2,1)S(1)} %fusion.28), channel_id=1, source_target_pairs={{0,16},{16,0},{1,17},{17,1},{2,18},{18,2},{3,19},{19,3},{4,20},{20... | collective-permute-start | bytes 1179656 | tf_op jit(solution)/shard_map/ppermute | solution.py:28
  163.0 20.7 %copy-start.12 = (bf16[1536,64]{0,1:T(8,128)(2,1)S(1)}, bf16[1536,64]{0,1:T(8,128)(2,1)}, u32[]{:S(2)}) copy-start(bf16[1536,64]{0,1:T(8,128)(2,1)} %param.22) | copy-start | bytes 589828
  164.7 19.5 %copy-start.16 = (f32[1,64,128]{2,1,0:T(8,128)S(1)}, f32[1,64,128]{2,1,0:T(8,128)}, u32[]{:S(2)}) copy-start(f32[1,64,128]{2,1,0:T(8,128)} %param.23) | copy-start | bytes 98308
Sparse Core Ops, SparseCore 0:
  122.6 36.9 reduce-scatter.3
